TPU v7x, 128 devices: a whole 4x4x4 slice. The times are simulated.
128 devices in a mesh: row: 8 (over x, z_lo), col: 16 (over z_hi, y, core).
Axes of the slice: x: 4, y: 4, z: 4 (z_hi: 2, z_lo: 2; z = z_hi * 2 + z_lo), core: 2. Of those that a mesh axis runs over, the one named last changes fastest.
Arguments:
- features: bfloat16 [65536, 256], P(('row', 'col')), may hold values from -6 to 6
- weight: bfloat16 [256, 256], replicated, may hold values from -0.375 to 0.375
- tile_values: bfloat16 [8, 16, 192, 128, 128], P('row', 'col'), may hold values from -0.078125 to 0.078125
- tile_coords: int32 [8, 16, 192, 2], P('row', 'col'), may hold values from 0 to 63, as said below
- tile_counts: int32 [8, 16], P('row', 'col'), may hold values from 48 to 192, as said below
- out_grad: bfloat16 [65536, 256], P(('row', 'col')), may hold values from -6 to 6
Outputs:
- activated: bfloat16 [65536, 256], P(('row', 'col'))
- weight_grad: float32 [256, 256], replicated
- feature_grad: bfloat16 [65536, 256], P(('row', 'col'))
Inputs may be any that keep to these rules, and one draw needn't show every extreme that they name: `tile_coords`: within one block the slots name distinct tiles; tile rows are below 64 and tile columns below 32. `tile_counts`: slots at or past a block's count are not part of the adjacency. Some block has 192 live slots.
All inputs are finite; a program needn't handle non-finite values.
Results may differ from a plain program's by a relative error of at most 0.006.
Values may be sent and summed in bfloat16 or wider, within the bound.
A program may use at most 192 MiB of HBM per device.

v0:
```python
import jax
import jax.numpy as jnp
from jax import lax
from jax.sharding import PartitionSpec as P


def silu_grad(value):
    sigma = jax.nn.sigmoid(value)
    return sigma * (1.0 + value * (1.0 - sigma))


def spread(tile_set, coords, count, source, out_tiles, transposed):
    tile_size = tile_set.shape[1]
    feature_width = source.shape[1]
    source_tiles = source.reshape(-1, tile_size, feature_width)
    if transposed:
        taken = coords[:, 0]
        placed = coords[:, 1]
    else:
        taken = coords[:, 1]
        placed = coords[:, 0]
    slot_count = tile_set.shape[0]
    block_size = min(128, slot_count)
    summed = jnp.zeros((out_tiles, tile_size, feature_width), jnp.float32)
    for first_slot in range(0, slot_count, block_size):
        last_slot = min(first_slot + block_size, slot_count)
        picked = source_tiles[taken[first_slot:last_slot]]
        if transposed:
            product = jnp.einsum(
                "kij,kif->kjf",
                tile_set[first_slot:last_slot],
                picked,
                preferred_element_type=jnp.float32,
            )
        else:
            product = jnp.einsum(
                "kij,kjf->kif",
                tile_set[first_slot:last_slot],
                picked,
                preferred_element_type=jnp.float32,
            )
        slot_ids = jnp.arange(first_slot, last_slot, dtype=jnp.int32)
        segment_ids = jnp.where(slot_ids < count, placed[first_slot:last_slot], out_tiles)
        summed = summed + jax.ops.segment_sum(product, segment_ids, num_segments=out_tiles)
    return summed.reshape(out_tiles * tile_size, feature_width)


def body(features, weight, tile_values, tile_coords, tile_counts, out_grad):
    tile_set = tile_values[0, 0]
    coords = tile_coords[0, 0]
    count = tile_counts[0, 0]
    node_rows = features.shape[0]
    tile_size = tile_set.shape[1]
    row_devices = lax.axis_size("row")
    col_devices = lax.axis_size("col")
    row_tiles = col_devices * node_rows // tile_size
    col_tiles = row_devices * node_rows // tile_size
    scaling = float(node_rows * row_devices * col_devices) ** (-0.5)
    column_owned = lax.all_gather(features, "row", axis=0, tiled=True)
    partial_sums = spread(tile_set, coords, count, column_owned, row_tiles, False)
    share = lax.psum_scatter(partial_sums, "col", scatter_dimension=0, tiled=True).astype(
        jnp.bfloat16
    )
    pre = jnp.dot(share, weight, preferred_element_type=jnp.float32)
    activated = jax.nn.silu(pre).astype(jnp.bfloat16)
    pre_grad = (out_grad.astype(jnp.float32) * silu_grad(pre)).astype(jnp.bfloat16)
    weight_term = lax.dot_general(
        share, pre_grad, (((0,), (0,)), ((), ())), preferred_element_type=jnp.float32
    )
    weight_grad = lax.psum(weight_term, ("row", "col")) * scaling
    agg_grad = lax.dot_general(
        pre_grad, weight, (((1,), (1,)), ((), ())), preferred_element_type=jnp.float32
    ).astype(jnp.bfloat16)
    grad_source = lax.all_gather(agg_grad, "col", axis=0, tiled=True)
    pieces = spread(tile_set, coords, count, grad_source, col_tiles, True)
    feature_grad = lax.psum_scatter(pieces, "row", scatter_dimension=0, tiled=True).astype(
        jnp.bfloat16
    )
    return (activated, weight_grad, feature_grad)


def solution(mesh):
    return jax.shard_map(
        body,
        mesh=mesh,
        in_specs=(
            P(("row", "col"), None),
            P(),
            P("row", "col", None, None, None),
            P("row", "col", None, None),
            P("row", "col"),
            P(("row", "col"), None),
        ),
        out_specs=(P(("row", "col"), None), P(), P(("row", "col"), None)),
        check_vma=False,
    )
```

profile of v0, /device:TPU:1, one launch (start us, length us, event | category | flops | bytes accessed | tf_op | source)
XLA Modules:
  0.0 603.6 jit_solution(15885839796586882708)
XLA Ops:
  7.2 0.0 copy-start
  7.2 0.0 all-gather.3.cloned.1.call-start
  7.2 0.7 all-gather.3.cloned.1.call-update
  7.9 0.0 reduce-scatter.3.cloned.1.call-start
  8.6 0.8 fusion.18
  9.4 0.8 fusion.19
  10.2 52.0 %all-gather.3.cloned.1.call-done = bf16[4096,256]{1,0:T(8,128)(2,1)} async-done(((bf16[512,256]{1,0:T(8,128)(2,1)}), bf16[4096,256]{1,0:T(8,128)(2,1)}) %all-gather.3.cloned.1.call-update) | async-done | bytes 2097168 | tf_op jit(solution)/shard_map/all_gather | solution.py:59
  62.1 8.2 %gather_fusion = bf16[128,128,256]{2,1,0:T(8,128)(2,1)} fusion(bf16[32,128,256]{2,1,0:T(8,128)(2,1)} %bitcast.50, s32[1024]{0:T(1024)S(1)} %pad_clamp_fusion.3), kind=kCustom, calls=%fused_computation | custom fusion | bytes 16777728 | tf_op jit(solution)/shard_map/gather | solution.py:27
  70.3 12.7 %convolution_bitcast_fusion.1 = f32[128,128,256]{1,2,0:T(8,128)} fusion(bf16[128,128,256]{2,1,0:T(8,128)(2,1)} %gather_fusion, bf16[1,1,192,128,128]{4,3,2,1,0:T(8,128)(2,1)} %param.8), kind=kOutput, calls=%fused_computation.9 | convolution fusion | flops 1073741824 | bytes 29360128 | tf_op jit(solution)/shard_map/kij,kjf->kif/dot_general | solution.py:36
  83.0 0.0 copy-start.2
  83.0 17.6 %copy.14 = f32[128,128,256]{2,1,0:T(8,128)} copy(f32[128,128,256]{1,2,0:T(8,128)} %convolution_bitcast_fusion.1) | data formatting | bytes 33554432 | tf_op jit(solution)/shard_map/kij,kjf->kif/dot_general | solution.py:36
  100.6 0.0 copy-done.2
  100.6 2.7 gather_fusion.1
  103.3 7.4 %convolution_bitcast_fusion.3 = f32[64,128,256]{1,2,0:T(8,128)} fusion(bf16[64,128,256]{2,1,0:T(8,128)(2,1)} %gather_fusion.1, bf16[1,1,192,128,128]{4,3,2,1,0:T(8,128)(2,1)} %param.8), kind=kOutput, calls=%fused_computation.15 | convolution fusion | flops 536870912 | bytes 14680064 | tf_op jit(solution)/shard_map/kij,kjf->kif/dot_general | solution.py:36
  110.7 9.0 %copy.16 = f32[64,128,256]{2,1,0:T(8,128)} copy(f32[64,128,256]{1,2,0:T(8,128)} %convolution_bitcast_fusion.3) | data formatting | bytes 16777216 | tf_op jit(solution)/shard_map/kij,kjf->kif/dot_general | solution.py:36
  119.7 4.2 broadcast.54.clone
  123.9 37.7 %scatter_fusion = f32[64,128,256]{2,1,0:T(8,128)} fusion(f32[64,128,256]{2,1,0:T(8,128)} %broadcast.54.clone, s32[128]{0:T(128)S(1)} %get-tuple-element.12, f32[128,128,256]{2,1,0:T(8,128)} %copy.14), kind=kCustom, calls=%fused_computation.4 | custom fusion | flops 4194304 | bytes 50332160 | tf_op jit(solution)/shard_map/scatter-add | solution.py:44
  161.6 4.2 broadcast.54.clone.1
  165.9 17.7 %scatter_fusion.1 = f32[64,128,256]{2,1,0:T(8,128)} fusion(f32[64,128,256]{2,1,0:T(8,128)} %broadcast.54.clone.1, s32[64]{0:T(128)S(1)} %get-tuple-element.8, f32[64,128,256]{2,1,0:T(8,128)} %copy.16), kind=kCustom, calls=%fused_computation.5 | custom fusion | flops 2097152 | bytes 25166080 | tf_op jit(solution)/shard_map/scatter-add | solution.py:44
  183.5 11.1 %add.69 = f32[64,128,256]{2,1,0:T(8,128)} add(f32[64,128,256]{2,1,0:T(8,128)} %scatter_fusion, f32[64,128,256]{2,1,0:T(8,128)} %scatter_fusion.1) | non-fusion elementwise | flops 2097152 | bytes 25165824 | tf_op jit(solution)/shard_map/add | solution.py:44
  194.7 0.0 copy-start.3
  194.7 0.0 reduce-scatter.3.cloned.1.call-update
  194.7 0.2 all-gather.5.cloned.1.call-start
  194.9 105.9 %reduce-scatter.3.cloned.1.call-done = f32[512,256]{1,0:T(8,128)} async-done(((f32[8192,256]{1,0:T(8,128)}), f32[512,256]{1,0:T(8,128)}) %reduce-scatter.3.cloned.1.call-update) | async-done | bytes 524304 | tf_op jit(solution)/shard_map/reduce_scatter | solution.py:61
  300.9 0.0 copy-done
  300.9 0.0 copy-done.3
  300.9 2.1 multiply_convert_fusion
  303.0 1.0 convolution_convert_fusion
  304.0 0.0 all-gather.5.cloned.1.call-update
  304.0 0.0 all-reduce.2.cloned.1.call-start
  304.1 2.0 fusion.8
  306.1 0.0 all-reduce.2.cloned.1.call-update
  306.1 0.0 reduce-scatter.5.cloned.1.call-start
  306.2 54.1 %all-gather.5.cloned.1.call-done = bf16[8192,256]{1,0:T(8,128)(2,1)} async-done(((bf16[512,256]{1,0:T(8,128)(2,1)}), bf16[8192,256]{1,0:T(8,128)(2,1)}) %all-gather.5.cloned.1.call-update) | async-done | bytes 4194320 | tf_op jit(solution)/shard_map/all_gather | solution.py:74
  360.3 8.7 %gather_fusion.2 = bf16[128,128,256]{2,1,0:T(8,128)(2,1)} fusion(bf16[64,128,256]{2,1,0:T(8,128)(2,1)} %bitcast.52, s32[1024]{0:T(1024)S(1)} %pad_clamp_fusion.1), kind=kCustom, calls=%fused_computation.2 | custom fusion | bytes 16777728 | tf_op jit(solution)/shard_map/gather | solution.py:27
  369.1 12.7 %convolution_bitcast_fusion = f32[128,128,256]{1,2,0:T(8,128)} fusion(bf16[128,128,256]{2,1,0:T(8,128)(2,1)} %gather_fusion.2, bf16[1,1,192,128,128]{4,3,2,1,0:T(8,128)(2,1)} %param.8), kind=kOutput, calls=%fused_computation.8 | convolution fusion | flops 1073741824 | bytes 29360128 | tf_op jit(solution)/shard_map/kij,kif->kjf/dot_general | solution.py:29
  381.8 5.0 gather_fusion.3
  386.8 7.4 %convolution_bitcast_fusion.2 = f32[64,128,256]{1,2,0:T(8,128)} fusion(bf16[64,128,256]{2,1,0:T(8,128)(2,1)} %gather_fusion.3, bf16[1,1,192,128,128]{4,3,2,1,0:T(8,128)(2,1)} %param.8), kind=kOutput, calls=%fused_computation.14 | convolution fusion | flops 536870912 | bytes 14680064 | tf_op jit(solution)/shard_map/kij,kif->kjf/dot_general | solution.py:29
  394.1 17.5 %copy.18 = f32[128,128,256]{2,1,0:T(8,128)} copy(f32[128,128,256]{1,2,0:T(8,128)} %convolution_bitcast_fusion) | data formatting | bytes 33554432 | tf_op jit(solution)/shard_map/kij,kif->kjf/dot_general | solution.py:29
  411.6 9.0 %copy.20 = f32[64,128,256]{2,1,0:T(8,128)} copy(f32[64,128,256]{1,2,0:T(8,128)} %convolution_bitcast_fusion.2) | data formatting | bytes 16777216 | tf_op jit(solution)/shard_map/kij,kif->kjf/dot_general | solution.py:29
  420.6 2.4 broadcast.58.clone
  423.1 37.5 %scatter_fusion.2 = f32[32,128,256]{2,1,0:T(8,128)} fusion(f32[32,128,256]{2,1,0:T(8,128)} %broadcast.58.clone, s32[128]{0:T(128)S(1)} %get-tuple-element.11, f32[128,128,256]{2,1,0:T(8,128)} %copy.18), kind=kCustom, calls=%fused_computation.6 | custom fusion | flops 4194304 | bytes 50332160 | tf_op jit(solution)/shard_map/scatter-add | solution.py:44
  460.6 2.4 broadcast.58.clone.1
  463.0 0.0 copy-start.1
  463.0 17.6 %scatter_fusion.3 = f32[32,128,256]{2,1,0:T(8,128)} fusion(f32[32,128,256]{2,1,0:T(8,128)} %broadcast.58.clone.1, s32[64]{0:T(128)S(1)} %get-tuple-element.7, f32[64,128,256]{2,1,0:T(8,128)} %copy.20), kind=kCustom, calls=%fused_computation.7 | custom fusion | flops 2097152 | bytes 25166080 | tf_op jit(solution)/shard_map/scatter-add | solution.py:44
  480.6 6.2 %add.74 = f32[32,128,256]{2,1,0:T(8,128)} add(f32[32,128,256]{2,1,0:T(8,128)} %scatter_fusion.2, f32[32,128,256]{2,1,0:T(8,128)} %scatter_fusion.3) | non-fusion elementwise | flops 1048576 | bytes 12582912 | tf_op jit(solution)/shard_map/add | solution.py:44
  486.8 0.0 reduce-scatter.5.cloned.1.call-update
  486.9 18.4 %all-reduce.2.cloned.1.call-done = f32[256,256]{1,0:T(8,128)} async-done(((f32[256,256]{1,0:T(8,128)}), f32[256,256]{1,0:T(8,128)}) %all-reduce.2.cloned.1.call-update) | async-done | bytes 262160 | tf_op jit(solution)/shard_map/psum | solution.py:70
  505.3 1.7 broadcast_multiply_fusion
  507.0 88.4 %reduce-scatter.5.cloned.1.call-done = f32[512,256]{1,0:T(8,128)} async-done(((f32[4096,256]{1,0:T(8,128)}), f32[512,256]{1,0:T(8,128)}) %reduce-scatter.5.cloned.1.call-update) | async-done | bytes 524304 | tf_op jit(solution)/shard_map/reduce_scatter | solution.py:76
  595.3 1.8 convert_element_type.23
  597.1 0.0 copy-done.1
  (4 shorter events, 0.0 us)
Async XLA Ops:
  7.2 293.7 %copy-start = (bf16[256,256]{1,0:T(8,128)(2,1)S(1)}, bf16[256,256]{1,0:T(8,128)(2,1)}, u32[]{:S(2)}) copy-start(bf16[256,256]{1,0:T(8,128)(2,1)} %param.7) | copy-start | bytes 393220
  7.2 55.0 %all-gather.3.cloned.1.call-start = ((), (), s32[]{:S(2)}) async-start(), calls=%async_computation.2 | async-start | bytes 2359296 | tf_op jit(solution)/shard_map/all_gather | solution.py:59
  7.9 293.0 %reduce-scatter.3.cloned.1.call-start = ((), (), s32[]{:S(2)}) async-start(), calls=%async_computation.3 | async-start | bytes 8912896 | tf_op jit(solution)/shard_map/reduce_scatter | solution.py:61
  83.0 17.6 %copy-start.2 = (bf16[4096,256]{1,0:T(8,128)(2,1)S(1)}, bf16[4096,256]{1,0:T(8,128)(2,1)}, u32[]{:S(2)}) copy-start(bf16[4096,256]{1,0:T(8,128)(2,1)} %all-gather.3.cloned.1.call-done) | copy-start | bytes 6291460
  194.7 106.2 %copy-start.3 = (bf16[512,256]{1,0:T(8,128)(2,1)S(1)}, bf16[512,256]{1,0:T(8,128)(2,1)}, u32[]{:S(2)}) copy-start(bf16[512,256]{1,0:T(8,128)(2,1)} %param.11) | copy-start | bytes 786436
  194.7 165.6 %all-gather.5.cloned.1.call-start = ((), (), s32[]{:S(2)}) async-start(), calls=%async_computation.5 | async-start | bytes 4456448 | tf_op jit(solution)/shard_map/all_gather | solution.py:74
  304.0 201.3 %all-reduce.2.cloned.1.call-start = ((), (), s32[]{:S(2)}) async-start(), calls=%async_computation.4 | async-start | bytes 524288 | tf_op jit(solution)/shard_map/psum | solution.py:70
  306.1 289.2 %reduce-scatter.5.cloned.1.call-start = ((), (), s32[]{:S(2)}) async-start(), calls=%async_computation.6 | async-start | bytes 4718592 | tf_op jit(solution)/shard_map/reduce_scatter | solution.py:76
  463.0 134.1 %copy-start.1 = (bf16[256,256]{1,0:T(8,128)(2,1)S(1)}, bf16[256,256]{1,0:T(8,128)(2,1)}, u32[]{:S(2)}) copy-start(bf16[256,256]{1,0:T(8,128)(2,1)} %param.7) | copy-start | bytes 393220
Sparse Core Ops, SparseCore 0:
  9.7 52.4 all-gather.2
  194.8 106.0 reduce-scatter.2
  304.1 56.1 all-gather.4
  365.5 139.7 all-reduce.1
  507.5 87.7 reduce-scatter.4
where the time goes:
time: 605 us; the launch traced here: 604 us
  waiting for transfers between devices  320 us (53%)
  other arithmetic  133 us (22%)
  local copies, waits for them, and re-layouts  91.1 us (15%)
  matrix products  45.3 us (7%)
  between operations  14.5 us (2%)
    scatter-add x4, other arithmetic, spread(): jax.ops.segment_sum(product, segment_ids, num_segments=out_tiles)  110 us
    reduce_scatter x1, waiting for transfers between devices, body(): lax.psum_scatter(partial_sums, 'col', scatter_dimension=0, tiled=True)  106 us
    reduce_scatter x1, waiting for transfers between devices, body(): lax.psum_scatter(pieces, 'row', scatter_dimension=0, tiled=True)  88.4 us
    all_gather x1, waiting for transfers between devices, body(): grad_source = lax.all_gather(agg_grad, 'col', axis=0, tiled=True)  54.1 us
    all_gather x1, waiting for transfers between devices, body(): column_owned = lax.all_gather(features, 'row', axis=0, tiled=True)  52 us
    dot_general x2, local copies, waits for them, and re-layouts, spread(): jnp.einsum('kij,kjf->kif', tile_set[first_slot:last_slot], picked, prefer...  26.6 us
    dot_general x2, local copies, waits for them, and re-layouts, spread(): jnp.einsum('kij,kif->kjf', tile_set[first_slot:last_slot], picked, prefer...  26.5 us
    gather x4, local copies, waits for them, and re-layouts, spread(): picked = source_tiles[taken[first_slot:last_slot]]  24.6 us
  transfers between devices with their start and end apart: 5, of which 5 were waited for; matrix products, arithmetic and copies ran while one was open for 22% of the time, Pallas kernels for 0%

commit v1 on v0

v1 whole, which is shorter than its diff:
```python
import functools

import jax
import jax.numpy as jnp
from jax import lax
from jax.experimental import pallas as pl
from jax.experimental.pallas import tpu as pltpu
from jax.sharding import PartitionSpec as P

MESH = pl.DeviceIdType.MESH
TILE = 128
SLOTS = 192
ROW_TILES = 64
COL_TILES = 32
OWN = 4
HALF = 2
PREV_F, SRC_F, LAST_F = 0, SLOTS, 2 * SLOTS
PREV_B = 2 * SLOTS + ROW_TILES
SRC_B, LAST_B = PREV_B + SLOTS, PREV_B + 2 * SLOTS
R_FARP, R_NEARP_U, R_NEARP_D, R_FAR_U, R_FAR_D, R_NEAR_U, R_NEAR_D, R_PAIR = 0, 4, 8, 12, 14, 16, 20, 24
R_TILES = 28
F32 = jnp.float32
BF16 = jnp.bfloat16


def send(src, dst, ssem, rsem, device):
    copy = pltpu.make_async_remote_copy(
        src_ref=src, dst_ref=dst, send_sem=ssem, recv_sem=rsem, device_id=device, device_id_type=MESH
    )
    copy.start()
    return copy


def arrive(dst, ssem, rsem, device):
    pltpu.make_async_remote_copy(
        src_ref=dst, dst_ref=dst, send_sem=ssem, recv_sem=rsem, device_id=device, device_id_type=MESH
    ).wait_recv()


class Ring:
    def __init__(self, i, p, device, block):
        self.up, self.down, self.far = lax.rem(i + 1, 4), lax.rem(i + 3, 4), lax.rem(i + 2, 4)
        self.i, self.p, self.q = i, p, 1 - p
        self.d_up, self.d_down, self.d_pair = device(self.up, p), device(self.down, p), device(i, self.q)
        self.block = block


def gather(ring, buf, ss, rs, sent, landed=lambda name: None):
    i, p, q, up, down, far = ring.i, ring.p, ring.q, ring.up, ring.down, ring.far

    def part(i, p, first=0, count=OWN):
        return buf.at[pl.ds(ring.block(i, p) * OWN + first, count)]

    def go(n, what, device):
        sent.append(send(what, what, ss.at[n], rs.at[n], device))

    def got(n, what, device):
        arrive(what, ss.at[n], rs.at[n], device)

    go(0, part(i, p), ring.d_up)
    go(1, part(i, p), ring.d_down)
    go(2, part(i, p), ring.d_pair)
    landed((i, p))
    yield
    got(0, part(down, p), ring.d_down)
    go(3, part(down, p, 0, HALF), ring.d_up)
    got(1, part(up, p), ring.d_up)
    go(4, part(up, p, HALF, HALF), ring.d_down)
    got(2, part(i, q), ring.d_pair)
    go(5, part(i, q), ring.d_up)
    go(6, part(i, q), ring.d_down)
    landed((down, p))
    landed((up, p))
    landed((i, q))
    yield
    got(3, part(far, p, 0, HALF), ring.d_down)
    go(7, part(far, p, 0, HALF), ring.d_pair)
    got(4, part(far, p, HALF, HALF), ring.d_up)
    go(8, part(far, p, HALF, HALF), ring.d_pair)
    landed((far, p))
    yield
    got(5, part(down, q), ring.d_down)
    got(6, part(up, q), ring.d_up)
    landed((down, q))
    landed((up, q))
    got(7, part(far, q, 0, HALF), ring.d_pair)
    got(8, part(far, q, HALF, HALF), ring.d_pair)
    landed((far, q))
    yield


def reduce(ring, partial, out, sbuf, rbuf, ss, rs, sent):
    i, p, q, up, down, far = ring.i, ring.p, ring.q, ring.up, ring.down, ring.far

    def go(n, first, count, device):
        sent.append(
            send(sbuf.at[pl.ds(first, count)], rbuf.at[pl.ds(first, count)], ss.at[n], rs.at[n], device)
        )

    def got(n, first, count, device):
        arrive(rbuf.at[pl.ds(first, count)], ss.at[n], rs.at[n], device)

    def put(first, block, tiles=range(OWN), terms=()):
        for n, t in enumerate(tiles):
            total = partial(*block, t)
            for term in terms:
                total = total + rbuf[term + n].astype(F32)
            sbuf[first + n] = total.astype(BF16)

    put(R_FARP, (far, q))
    go(0, R_FARP, HALF, ring.d_pair)
    go(1, R_FARP + HALF, HALF, ring.d_pair)
    put(R_NEARP_U, (up, q))
    go(2, R_NEARP_U, OWN, ring.d_up)
    put(R_NEARP_D, (down, q))
    go(3, R_NEARP_D, OWN, ring.d_down)
    yield
    got(0, R_FARP, HALF, ring.d_pair)
    put(R_FAR_U, (far, p), (0, 1), (R_FARP,))
    go(4, R_FAR_U, HALF, ring.d_up)
    got(1, R_FARP + HALF, HALF, ring.d_pair)
    put(R_FAR_D, (far, p), (2, 3), (R_FARP + HALF,))
    go(5, R_FAR_D, HALF, ring.d_down)
    yield
    got(2, R_NEARP_U, OWN, ring.d_down)
    got(3, R_NEARP_D, OWN, ring.d_up)
    put(R_PAIR, (i, q), range(OWN), (R_NEARP_U, R_NEARP_D))
    go(6, R_PAIR, OWN, ring.d_pair)
    yield
    got(4, R_FAR_U, HALF, ring.d_down)
    put(R_NEAR_U, (up, p), (0, 1), (R_FAR_U,))
    put(R_NEAR_U + HALF, (up, p), (2, 3))
    go(7, R_NEAR_U, OWN, ring.d_up)
    got(5, R_FAR_D, HALF, ring.d_up)
    put(R_NEAR_D, (down, p), (0, 1))
    put(R_NEAR_D + HALF, (down, p), (2, 3), (R_FAR_D,))
    go(8, R_NEAR_D, OWN, ring.d_down)
    yield
    got(6, R_PAIR, OWN, ring.d_pair)
    got(7, R_NEAR_U, OWN, ring.d_down)
    got(8, R_NEAR_D, OWN, ring.d_up)
    for t in range(OWN):
        total = partial(i, p, t)
        for term in (R_PAIR, R_NEAR_U, R_NEAR_D):
            total = total + rbuf[term + t].astype(F32)
        out(t, total)
    yield


def kernel(
    scaling, table, features, weight, tiles, out_grad, activated, weight_grad, feature_grad,
    T, S0, S1, F0, F1, CS0, CS1, CR0, CR1, AS0, AS1, AR0, AR1, G0, G1, BS0, BS1, BR0, BR1,
    AGG0, AGG1, PG, WT, WA, WP, WB, WC,
    tile_sem, gf_s, gf_r, cx_s, cx_r, rf_s, rf_r, gb_s, gb_r, co_s, co_r, rb_s, rb_r,
    wa_s, wa_r, wb_s, wb_r, wc_s, wc_r,
):
    S, F, CS, CR, AS, AR = (S0, S1), (F0, F1), (CS0, CS1), (CR0, CR1), (AS0, AS1), (AR0, AR1)
    G, BS, BR, AGG = (G0, G1), (BS0, BS1), (BR0, BR1), (AGG0, AGG1)
    row, col = lax.axis_index("row"), lax.axis_index("col")
    x, zl = row // 2, lax.rem(row, 2)
    zh, y, co = col // 8, lax.rem(col, 8) // 2, lax.rem(col, 2)
    row_ring = Ring(x, zl, lambda i, p: (i * 2 + p, col), lambda i, p: i * 2 + p)
    col_ring = Ring(y, zh, lambda i, p: (row, p * 8 + i * 2 + co), lambda i, p: p * 8 + i * 2 + co)
    partner = (row, zh * 8 + y * 2 + 1 - co)
    sent = []

    loads = []
    for n in range(4):
        span = pl.ds(n * (SLOTS // 4), SLOTS // 4)
        loads.append(pltpu.make_async_copy(tiles.at[span], T.at[span], tile_sem.at[n]))
        loads[-1].start()

    barrier = pltpu.get_barrier_semaphore()

    def greet_col(k, c):
        pl.semaphore_signal(barrier, inc=1, device_id=(row, lax.rem(col + k, 16)), device_id_type=MESH)
        return c

    def greet_row(k, c):
        pl.semaphore_signal(barrier, inc=1, device_id=(lax.rem(row + k, 8), col), device_id_type=MESH)
        return c

    lax.fori_loop(1, 16, greet_col, 0)
    lax.fori_loop(1, 8, greet_row, 0)
    for h in range(2):
        for t in range(OWN):
            F[h][row * OWN + t] = features[t * TILE:(t + 1) * TILE, h * TILE:(h + 1) * TILE]
        S[h][SLOTS] = jnp.zeros((TILE, TILE), F32)
    pl.semaphore_wait(barrier, 22)

    def spread(h, source, prev, src, contract, first=0, last=SLOTS):
        def step(k, c):
            term = lax.dot_general(
                T[k], source[table[src + k]], (((contract,), (0,)), ((), ())), preferred_element_type=F32
            )
            S[h][k] = S[h][table[prev + k]] + term
            return c

        lax.fori_loop(first, last, step, 0, unroll=16)

    def core_exchange(h):
        for b in range(8):
            for t in range(OWN):
                CS[h][b * OWN + t] = S[h][table[LAST_F + (b * 2 + 1 - co) * OWN + t]].astype(BF16)
        sent.append(send(CS[h], CR[h], cx_s.at[h], cx_r.at[h], partner))

    def forward_term(h, i, p, t):
        b = p * 4 + i
        return S[h][table[LAST_F + (b * 2 + co) * OWN + t]] + CR[h][b * OWN + t].astype(F32)

    def keep_aggregated(h, t, value):
        AGG[h][t * TILE:(t + 1) * TILE, :] = value.astype(BF16)

    gf = [gather(row_ring, F[h], gf_s.at[h], gf_r.at[h], sent) for h in range(2)]
    rf = [
        reduce(col_ring, functools.partial(forward_term, h), functools.partial(keep_aggregated, h),
               AS[h], AR[h], rf_s.at[h], rf_r.at[h], sent)
        for h in range(2)
    ]
    next(gf[0])
    next(gf[0])
    next(gf[1])
    next(gf[0])
    next(gf[1])
    for load in loads:
        load.wait()
    next(gf[0])
    spread(0, F[0], PREV_F, SRC_F, 1)
    core_exchange(0)
    next(gf[1])
    arrive(CR[0], cx_s.at[0], cx_r.at[0], partner)
    next(rf[0])
    next(gf[1])
    next(rf[0])
    spread(1, F[1], PREV_F, SRC_F, 1)
    core_exchange(1)
    next(rf[0])
    next(rf[0])
    arrive(CR[1], cx_s.at[1], cx_r.at[1], partner)
    next(rf[1])
    next(rf[1])
    next(rf[0])
    next(rf[1])
    next(rf[1])
    next(rf[1])

    def own_tile(t, c):
        rows = pl.ds(pl.multiple_of(t * TILE, TILE), TILE)
        pre = jnp.dot(AGG0[rows, :], weight[:TILE, :], preferred_element_type=F32)
        pre = pre + jnp.dot(AGG1[rows, :], weight[TILE:, :], preferred_element_type=F32)
        sigma = jax.nn.sigmoid(pre)
        activated[rows, :] = (pre * sigma).astype(BF16)
        grad = out_grad[rows, :].astype(F32) * (sigma * (1.0 + pre * (1.0 - sigma)))
        grad = grad.astype(BF16)
        PG[rows, :] = grad
        for h in range(2):
            back = lax.dot_general(
                grad, weight[h * TILE:(h + 1) * TILE, :], (((1,), (1,)), ((), ())), preferred_element_type=F32
            )
            G[h][col * OWN + t] = back.astype(BF16)
        return c

    lax.fori_loop(0, OWN, own_tile, 0, unroll=2)

    def to_partner(h):
        count = [0]

        def landed(place):
            what = G[h].at[pl.ds(col_ring.block(*place) * OWN, OWN)]
            n = count[0]
            count[0] += 1
            sent.append(send(what, what, co_s.at[h, n], co_r.at[h, n], partner))

        return landed

    def from_partner(h):
        r = col_ring
        places = [(r.i, r.p), (r.down, r.p), (r.up, r.p), (r.i, r.q), (r.far, r.p), (r.down, r.q), (r.up, r.q), (r.far, r.q)]
        for n, (i, p) in enumerate(places):
            arrive(G[h].at[pl.ds((p * 8 + i * 2 + 1 - co) * OWN, OWN)], co_s.at[h, n], co_r.at[h, n], partner)

    def backward_term(h, i, p, t):
        return S[h][table[LAST_B + (i * 2 + p) * OWN + t]]

    def keep_feature_grad(h, t, value):
        feature_grad[t * TILE:(t + 1) * TILE, h * TILE:(h + 1) * TILE] = value.astype(BF16)

    gb = [gather(col_ring, G[h], gb_s.at[h], gb_r.at[h], sent, to_partner(h)) for h in range(2)]
    rb = [
        reduce(row_ring, functools.partial(backward_term, h), functools.partial(keep_feature_grad, h),
               BS[h], BR[h], rb_s.at[h], rb_r.at[h], sent)
        for h in range(2)
    ]

    def weight_term():
        for h in range(2):
            WT[h * TILE:(h + 1) * TILE, :] = lax.dot_general(
                AGG[h][...], PG[...], (((0,), (0,)), ((), ())), preferred_element_type=F32
            )

        def go(k, c):
            to = lax.rem(col + k, 16)
            send(WT.at[pl.ds(to * 16, 16)], WA.at[col], wa_s.at[k], wa_r.at[k], (row, to))
            return c

        lax.fori_loop(1, 16, go, 0)

    def weight_row():
        WA[col] = WT[pl.ds(pl.multiple_of(col * 16, 16), 16), :]

        def got(k, c):
            fro = lax.rem(col + 16 - k, 16)
            arrive(WA.at[fro], wa_s.at[k], wa_r.at[k], (row, fro))
            return c

        lax.fori_loop(1, 16, got, 0)
        total = WA[0]
        for n in range(1, 16):
            total = total + WA[n]
        WP[...] = total
        WB[row] = total

        def go(k, c):
            to = lax.rem(row + k, 8)
            send(WP, WB.at[row], wb_s.at[k], wb_r.at[k], (to, col))
            return c

        lax.fori_loop(1, 8, go, 0)

    def weight_back():
        def got(k, c):
            fro = lax.rem(row + 8 - k, 8)
            arrive(WB.at[fro], wb_s.at[k], wb_r.at[k], (fro, col))
            return c

        lax.fori_loop(1, 8, got, 0)
        total = WB[0]
        for n in range(1, 8):
            total = total + WB[n]
        here = pl.ds(pl.multiple_of(col * 16, 16), 16)
        WC[here, :] = total * scaling

        def go(k, c):
            to = lax.rem(col + k, 16)
            send(WC.at[here], WC.at[here], wc_s.at[k], wc_r.at[k], (row, to))
            return c

        lax.fori_loop(1, 16, go, 0)

    def weight_end():
        def got(k, c):
            fro = lax.rem(col + 16 - k, 16)
            arrive(WC.at[pl.ds(fro * 16, 16)], wc_s.at[k], wc_r.at[k], (row, fro))
            return c

        lax.fori_loop(1, 16, got, 0)
        weight_grad[...] = WC[...]

    next(gb[0])
    weight_term()
    next(gb[0])
    next(gb[1])
    next(gb[0])
    next(gb[1])
    next(gb[0])
    weight_row()
    from_partner(0)
    spread(0, G[0], PREV_B, SRC_B, 0)
    next(gb[1])
    next(rb[0])
    weight_back()
    next(gb[1])
    next(rb[0])
    from_partner(1)
    spread(1, G[1], PREV_B, SRC_B, 0)
    next(rb[0])
    next(rb[1])
    next(rb[0])
    next(rb[1])
    next(rb[0])
    next(rb[1])
    next(rb[1])
    weight_end()
    next(rb[1])

    for copy in sent:
        copy.wait_send()

    def gone_col(k, c):
        pltpu.make_async_remote_copy(
            src_ref=WP, dst_ref=WP, send_sem=wa_s.at[k], recv_sem=wa_r.at[k], device_id=partner, device_id_type=MESH
        ).wait_send()
        pltpu.make_async_remote_copy(
            src_ref=WP, dst_ref=WP, send_sem=wc_s.at[k], recv_sem=wc_r.at[k], device_id=partner, device_id_type=MESH
        ).wait_send()
        return c

    def gone_row(k, c):
        pltpu.make_async_remote_copy(
            src_ref=WP, dst_ref=WP, send_sem=wb_s.at[k], recv_sem=wb_r.at[k], device_id=partner, device_id_type=MESH
        ).wait_send()
        return c

    lax.fori_loop(1, 16, gone_col, 0)
    lax.fori_loop(1, 8, gone_row, 0)


def links(place, live, groups):
    slot = jnp.arange(SLOTS, dtype=jnp.int32)
    before = (place[None, :] == place[:, None]) & (slot[None, :] < slot[:, None]) & live[None, :]
    previous = jnp.max(jnp.where(before, slot[None, :], -1), axis=1)
    group = jnp.arange(groups, dtype=jnp.int32)
    inside = (place[None, :] == group[:, None]) & live[None, :]
    last = jnp.max(jnp.where(inside, slot[None, :], -1), axis=1)
    return jnp.where(previous < 0, SLOTS, previous), jnp.where(last < 0, SLOTS, last)


def body(scaling, features, weight, tile_values, tile_coords, tile_counts, out_grad):
    coords = tile_coords[0, 0]
    live = jnp.arange(SLOTS, dtype=jnp.int32) < tile_counts[0, 0]
    tile_row, tile_col = coords[:, 0], coords[:, 1]
    prev_f, last_f = links(tile_row, live, ROW_TILES)
    prev_b, last_b = links(tile_col, live, COL_TILES)
    table = jnp.concatenate(
        [prev_f, jnp.where(live, tile_col, 0), last_f, prev_b, jnp.where(live, tile_row, 0), last_b]
    )
    rows, width = features.shape
    vmem = pl.BlockSpec(memory_space=pltpu.VMEM)
    tile = (TILE, TILE)

    def twice(count, kind=BF16):
        return [pltpu.VMEM((count,) + tile, kind)] * 2

    dma = pltpu.SemaphoreType.DMA
    return pl.pallas_call(
        functools.partial(kernel, scaling),
        out_shape=(
            jax.ShapeDtypeStruct((rows, width), BF16),
            jax.ShapeDtypeStruct((width, width), F32),
            jax.ShapeDtypeStruct((rows, width), BF16),
        ),
        in_specs=[
            pl.BlockSpec(memory_space=pltpu.SMEM), vmem, vmem, pl.BlockSpec(memory_space=pl.ANY), vmem,
        ],
        out_specs=(vmem, vmem, vmem),
        scratch_shapes=[
            pltpu.VMEM((SLOTS,) + tile, BF16),
            *twice(SLOTS + 1, F32), *twice(COL_TILES), *twice(32), *twice(32), *twice(R_TILES), *twice(R_TILES),
            *twice(ROW_TILES), *twice(R_TILES), *twice(R_TILES),
            pltpu.VMEM((rows, TILE), BF16), pltpu.VMEM((rows, TILE), BF16), pltpu.VMEM((rows, width), BF16),
            pltpu.VMEM((width, width), F32), pltpu.VMEM((16, 16, width), F32), pltpu.VMEM((16, width), F32),
            pltpu.VMEM((8, 16, width), F32), pltpu.VMEM((width, width), F32),
            dma((4,)), dma((2, 9)), dma((2, 9)), dma((2,)), dma((2,)), dma((2, 9)), dma((2, 9)),
            dma((2, 9)), dma((2, 9)), dma((2, 8)), dma((2, 8)), dma((2, 9)), dma((2, 9)),
            dma((16,)), dma((16,)), dma((8,)), dma((8,)), dma((16,)), dma((16,)),
        ],
        compiler_params=pltpu.CompilerParams(
            collective_id=0, has_side_effects=True, vmem_limit_bytes=62 << 20
        ),
    )(table, features, weight, tile_values[0, 0], out_grad)


def solution(mesh):
    nodes = 512 * mesh.shape["row"] * mesh.shape["col"]
    return jax.shard_map(
        functools.partial(body, float(nodes) ** -0.5),
        mesh=mesh,
        in_specs=(
            P(("row", "col"), None), P(), P("row", "col", None, None, None), P("row", "col", None, None),
            P("row", "col"), P(("row", "col"), None),
        ),
        out_specs=(P(("row", "col"), None), P(), P(("row", "col"), None)),
        check_vma=False,
    )
```

time: 605 us -> 115 us (0.19)
  waiting for transfers between devices: 320 us -> 0 us
  other arithmetic: 133 us -> 0.52 us
  Pallas kernels: 0 us -> 106 us
  local copies, waits for them, and re-layouts: 91.1 us -> 6.44 us
  matrix products: 45.3 us -> 0 us
  between operations: 14.5 us -> 1.32 us
    reduce_scatter x2 -> x0, waiting for transfers between devices: 194 us -> none  [the longest x1 106 us: body(): lax.psum_scatter(partial_sums, 'col', scatter_dimension=0, tiled=True)]
    scatter-add x4 -> x0, other arithmetic: 110 us -> none  [spread(): jax.ops.segment_sum(product, segment_ids, num_segments=out_tiles)]
    all_gather x2 -> x0, waiting for transfers between devices: 106 us -> none  [the longest x1 54.1 us: body(): grad_source = lax.all_gather(agg_grad, 'col', axis=0, tiled=True)]
    pallas_call x0 -> x1, Pallas kernels: none -> 106 us  [body(): pl.pallas_call(functools.partial(kernel, scaling), out_shape=(jax.ShapeDt...]
    dot_general x4 -> x0, local copies, waits for them, and re-layouts: 53.1 us -> none  [the longest x2 26.6 us: spread(): jnp.einsum('kij,kjf->kif', tile_set[first_slot:last_slot], picked, prefer...]
    dot_general x7 -> x0, matrix products: 45.3 us -> none  [the longest x2 20.1 us: spread(): jnp.einsum('kij,kif->kjf', tile_set[first_slot:last_slot], picked, prefer...]
    gather x4 -> x0, local copies, waits for them, and re-layouts: 24.6 us -> none  [spread(): picked = source_tiles[taken[first_slot:last_slot]]]
    psum x1 -> x0, waiting for transfers between devices: 18.4 us -> none  [body(): weight_grad = lax.psum(weight_term, ('row', 'col')) * scaling]
  transfers between devices with their start and end apart: 5 -> 0, of which waited for: 5 -> 0; matrix products, arithmetic and copies ran while one was open for 22% -> 0% of each run, Pallas kernels for 0% -> 0%
where the time goes in v1:
time: 115 us; the launch traced here: 114 us
  Pallas kernels  106 us (92%)
  local copies, waits for them, and re-layouts  6.44 us (6%)
  between operations  1.32 us (1%)
    pallas_call x1, Pallas kernels, body(): pl.pallas_call(functools.partial(kernel, scaling), out_shape=(jax.ShapeDt...  106 us
    unnamed x3, local copies, waits for them, and re-layouts  5.01 us

profile of v1, /device:TPU:1, one launch (start us, length us, event | category | flops | bytes accessed | tf_op | source)
XLA Modules:
  0.0 114.2 jit_solution(17030846635901053125)
XLA Ops:
  1.3 0.8 fusion.6
  2.1 0.1 select_reduce_fusion.3
  2.2 0.1 select_reduce_fusion.2
  2.3 0.2 select_reduce_fusion
  2.6 0.7 concatenate.3.table
  3.3 105.9 %shard_map.85 = (bf16[512,256]{1,0:T(8,128)(2,1)}, f32[256,256]{1,0:T(8,128)}, bf16[512,256]{1,0:T(8,128)(2,1)}) custom-call(s32[864]{0:T(1024)} %concatenate.3.table, bf16[512,256]{1,0:T(8,128)(2,1)} %features.1, bf16[256,256]{1,0:T(8,128)(2,1)} %weight.1, bf16[192,128,128]{2,1,0:T(8,128)(2,1)} %bitcast.7, bf16[512,256]{1,0:T(8,128)(2,1)} %out_grad.1), custom_call_target="tpu_custom_call" | custom-call | tf_op jit(solution)/shard_map/pallas_call | solution.py:435
  109.2 1.7 %copy.13 = bf16[512,256]{1,0:T(8,128)(2,1)} copy(bf16[512,256]{1,0:T(8,128)(2,1)} %get-tuple-element.14) | data formatting | bytes 524288
  110.8 1.7 %copy.14 = f32[256,256]{1,0:T(8,128)} copy(f32[256,256]{1,0:T(8,128)} %get-tuple-element.15) | data formatting | bytes 524288
  112.5 1.7 %copy.15 = bf16[512,256]{1,0:T(8,128)(2,1)} copy(bf16[512,256]{1,0:T(8,128)(2,1)} %get-tuple-element.16) | data formatting | bytes 524288
  (5 shorter events, 0.0 us)

commit v2 on v1

--- a/solution.py
+++ b/solution.py
@@ -14,9 +14,8 @@
 COL_TILES = 32
 OWN = 4
 HALF = 2
-PREV_F, SRC_F, LAST_F = 0, SLOTS, 2 * SLOTS
-PREV_B = 2 * SLOTS + ROW_TILES
-SRC_B, LAST_B = PREV_B + SLOTS, PREV_B + 2 * SLOTS
+WIDE = 256
+PREV_F, SRC_F, LAST_F, PREV_B, SRC_B, LAST_B = range(6)
 R_FARP, R_NEARP_U, R_NEARP_D, R_FAR_U, R_FAR_D, R_NEAR_U, R_NEAR_D, R_PAIR = 0, 4, 8, 12, 14, 16, 20, 24
 R_TILES = 28
 F32 = jnp.float32
@@ -37,6 +36,11 @@
     ).wait_recv()
 
 
+def run(steps, count):
+    for _ in range(count):
+        next(steps)
+
+
 class Ring:
     def __init__(self, i, p, device, block):
         self.up, self.down, self.far = lax.rem(i + 1, 4), lax.rem(i + 3, 4), lax.rem(i + 2, 4)
@@ -57,34 +61,40 @@
     def got(n, what, device):
         arrive(what, ss.at[n], rs.at[n], device)
 
-    go(0, part(i, p), ring.d_up)
-    go(1, part(i, p), ring.d_down)
-    go(2, part(i, p), ring.d_pair)
+    go(0, part(i, p, 0, HALF), ring.d_up)
+    go(1, part(i, p, HALF, HALF), ring.d_down)
+    go(4, part(i, p), ring.d_pair)
+    go(2, part(i, p, HALF, HALF), ring.d_up)
+    go(3, part(i, p, 0, HALF), ring.d_down)
     landed((i, p))
     yield
-    got(0, part(down, p), ring.d_down)
-    go(3, part(down, p, 0, HALF), ring.d_up)
-    got(1, part(up, p), ring.d_up)
-    go(4, part(up, p, HALF, HALF), ring.d_down)
-    got(2, part(i, q), ring.d_pair)
-    go(5, part(i, q), ring.d_up)
-    go(6, part(i, q), ring.d_down)
+    got(0, part(down, p, 0, HALF), ring.d_down)
+    go(5, part(down, p, 0, HALF), ring.d_up)
+    got(1, part(up, p, HALF, HALF), ring.d_up)
+    go(6, part(up, p, HALF, HALF), ring.d_down)
+    yield
+    got(4, part(i, q), ring.d_pair)
+    go(7, part(i, q), ring.d_up)
+    go(8, part(i, q), ring.d_down)
+    landed((i, q))
+    got(2, part(down, p, HALF, HALF), ring.d_down)
     landed((down, p))
+    got(3, part(up, p, 0, HALF), ring.d_up)
     landed((up, p))
-    landed((i, q))
-    yield
-    got(3, part(far, p, 0, HALF), ring.d_down)
-    go(7, part(far, p, 0, HALF), ring.d_pair)
-    got(4, part(far, p, HALF, HALF), ring.d_up)
-    go(8, part(far, p, HALF, HALF), ring.d_pair)
+    yield
+    got(5, part(far, p, 0, HALF), ring.d_down)
+    go(9, part(far, p, 0, HALF), ring.d_pair)
+    got(6, part(far, p, HALF, HALF), ring.d_up)
+    go(10, part(far, p, HALF, HALF), ring.d_pair)
     landed((far, p))
     yield
-    got(5, part(down, q), ring.d_down)
-    got(6, part(up, q), ring.d_up)
+    got(7, part(down, q), ring.d_down)
     landed((down, q))
+    got(8, part(up, q), ring.d_up)
     landed((up, q))
-    got(7, part(far, q, 0, HALF), ring.d_pair)
-    got(8, part(far, q, HALF, HALF), ring.d_pair)
+    yield
+    got(9, part(far, q, 0, HALF), ring.d_pair)
+    got(10, part(far, q, HALF, HALF), ring.d_pair)
     landed((far, q))
     yield
 
@@ -114,31 +124,35 @@
     go(2, R_NEARP_U, OWN, ring.d_up)
     put(R_NEARP_D, (down, q))
     go(3, R_NEARP_D, OWN, ring.d_down)
+    put(R_NEAR_U + HALF, (up, p), (2, 3))
+    go(4, R_NEAR_U + HALF, HALF, ring.d_up)
+    put(R_NEAR_D, (down, p), (0, 1))
+    go(5, R_NEAR_D, HALF, ring.d_down)
     yield
     got(0, R_FARP, HALF, ring.d_pair)
     put(R_FAR_U, (far, p), (0, 1), (R_FARP,))
-    go(4, R_FAR_U, HALF, ring.d_up)
+    go(6, R_FAR_U, HALF, ring.d_up)
     got(1, R_FARP + HALF, HALF, ring.d_pair)
     put(R_FAR_D, (far, p), (2, 3), (R_FARP + HALF,))
-    go(5, R_FAR_D, HALF, ring.d_down)
+    go(7, R_FAR_D, HALF, ring.d_down)
     yield
     got(2, R_NEARP_U, OWN, ring.d_down)
     got(3, R_NEARP_D, OWN, ring.d_up)
     put(R_PAIR, (i, q), range(OWN), (R_NEARP_U, R_NEARP_D))
-    go(6, R_PAIR, OWN, ring.d_pair)
-    yield
-    got(4, R_FAR_U, HALF, ring.d_down)
+    go(8, R_PAIR, OWN, ring.d_pair)
+    yield
+    got(6, R_FAR_U, HALF, ring.d_down)
     put(R_NEAR_U, (up, p), (0, 1), (R_FAR_U,))
-    put(R_NEAR_U + HALF, (up, p), (2, 3))
-    go(7, R_NEAR_U, OWN, ring.d_up)
-    got(5, R_FAR_D, HALF, ring.d_up)
-    put(R_NEAR_D, (down, p), (0, 1))
+    go(9, R_NEAR_U, HALF, ring.d_up)
+    got(7, R_FAR_D, HALF, ring.d_up)
     put(R_NEAR_D + HALF, (down, p), (2, 3), (R_FAR_D,))
-    go(8, R_NEAR_D, OWN, ring.d_down)
-    yield
-    got(6, R_PAIR, OWN, ring.d_pair)
-    got(7, R_NEAR_U, OWN, ring.d_down)
-    got(8, R_NEAR_D, OWN, ring.d_up)
+    go(10, R_NEAR_D + HALF, HALF, ring.d_down)
+    yield
+    got(4, R_NEAR_U + HALF, HALF, ring.d_down)
+    got(5, R_NEAR_D, HALF, ring.d_up)
+    got(8, R_PAIR, OWN, ring.d_pair)
+    got(9, R_NEAR_U, HALF, ring.d_down)
+    got(10, R_NEAR_D + HALF, HALF, ring.d_up)
     for t in range(OWN):
         total = partial(i, p, t)
         for term in (R_PAIR, R_NEAR_U, R_NEAR_D):
@@ -147,11 +161,31 @@
     yield
 
 
+def make_table(coords, count, out):
+    first = lax.broadcasted_iota(jnp.int32, (WIDE, WIDE), 0)
+    second = lax.broadcasted_iota(jnp.int32, (WIDE, WIDE), 1)
+    out[...] = jnp.zeros_like(out)
+    pad = jnp.zeros((1, WIDE - SLOTS), jnp.int32)
+    lane = lax.broadcasted_iota(jnp.int32, (1, WIDE), 1)
+    for group, source, rows in ((0, 1, (PREV_F, SRC_F, LAST_F)), (1, 0, (PREV_B, SRC_B, LAST_B))):
+        place = jnp.concatenate([coords[group:group + 1, :], pad], axis=1)
+        taken = jnp.concatenate([coords[source:source + 1, :], pad], axis=1)
+        along = jnp.broadcast_to(place, (WIDE, WIDE))
+        across = along.T
+        before = jnp.where((across == along) & (first < second) & (first < count), first, -1)
+        previous = jnp.max(before, axis=0, keepdims=True)
+        inside = jnp.where((across == second) & (first < count), first, -1)
+        last = jnp.max(inside, axis=0, keepdims=True)
+        out[rows[0]:rows[0] + 1, :] = jnp.where(previous < 0, SLOTS, previous)
+        out[rows[1]:rows[1] + 1, :] = jnp.where(lane < count, taken, 0)
+        out[rows[2]:rows[2] + 1, :] = jnp.where(last < 0, SLOTS, last)
+
+
 def kernel(
-    scaling, table, features, weight, tiles, out_grad, activated, weight_grad, feature_grad,
+    scaling, count, coords, features, weight, tiles, out_grad, activated, weight_grad, feature_grad,
     T, S0, S1, F0, F1, CS0, CS1, CR0, CR1, AS0, AS1, AR0, AR1, G0, G1, BS0, BS1, BR0, BR1,
     AGG0, AGG1, PG, WT, WA, WP, WB, WC,
-    tile_sem, gf_s, gf_r, cx_s, cx_r, rf_s, rf_r, gb_s, gb_r, co_s, co_r, rb_s, rb_r,
+    TABLE, table, table_sem, tile_sem, gf_s, gf_r, cx_s, cx_r, rf_s, rf_r, gb_s, gb_r, co_s, co_r, rb_s, rb_r,
     wa_s, wa_r, wb_s, wb_r, wc_s, wc_r,
 ):
     S, F, CS, CR, AS, AR = (S0, S1), (F0, F1), (CS0, CS1), (CR0, CR1), (AS0, AS1), (AR0, AR1)
@@ -186,27 +220,30 @@
         for t in range(OWN):
             F[h][row * OWN + t] = features[t * TILE:(t + 1) * TILE, h * TILE:(h + 1) * TILE]
         S[h][SLOTS] = jnp.zeros((TILE, TILE), F32)
+    make_table(coords, count[0, 0], TABLE)
+    table_copy = pltpu.make_async_copy(TABLE, table, table_sem)
+    table_copy.start()
     pl.semaphore_wait(barrier, 22)
 
     def spread(h, source, prev, src, contract, first=0, last=SLOTS):
         def step(k, c):
             term = lax.dot_general(
-                T[k], source[table[src + k]], (((contract,), (0,)), ((), ())), preferred_element_type=F32
+                T[k], source[table[src, k]], (((contract,), (0,)), ((), ())), preferred_element_type=F32
             )
-            S[h][k] = S[h][table[prev + k]] + term
-            return c
-
-        lax.fori_loop(first, last, step, 0, unroll=16)
+            S[h][k] = S[h][table[prev, k]] + term
+            return c
+
+        lax.fori_loop(first, last, step, 0, unroll=32)
 
     def core_exchange(h):
         for b in range(8):
             for t in range(OWN):
-                CS[h][b * OWN + t] = S[h][table[LAST_F + (b * 2 + 1 - co) * OWN + t]].astype(BF16)
+                CS[h][b * OWN + t] = S[h][table[LAST_F, (b * 2 + 1 - co) * OWN + t]].astype(BF16)
         sent.append(send(CS[h], CR[h], cx_s.at[h], cx_r.at[h], partner))
 
     def forward_term(h, i, p, t):
         b = p * 4 + i
-        return S[h][table[LAST_F + (b * 2 + co) * OWN + t]] + CR[h][b * OWN + t].astype(F32)
+        return S[h][table[LAST_F, (b * 2 + co) * OWN + t]] + CR[h][b * OWN + t].astype(F32)
 
     def keep_aggregated(h, t, value):
         AGG[h][t * TILE:(t + 1) * TILE, :] = value.astype(BF16)
@@ -217,32 +254,31 @@
                AS[h], AR[h], rf_s.at[h], rf_r.at[h], sent)
         for h in range(2)
     ]
-    next(gf[0])
-    next(gf[0])
-    next(gf[1])
-    next(gf[0])
-    next(gf[1])
+    run(gf[0], 3)
+    run(gf[1], 1)
+    run(gf[0], 2)
+    run(gf[1], 2)
+    run(gf[0], 1)
+    table_copy.wait()
     for load in loads:
         load.wait()
-    next(gf[0])
-    spread(0, F[0], PREV_F, SRC_F, 1)
+    spread(0, F[0], PREV_F, SRC_F, 1, 0, 128)
+    run(gf[1], 1)
+    spread(0, F[0], PREV_F, SRC_F, 1, 128)
     core_exchange(0)
-    next(gf[1])
+    run(gf[1], 1)
     arrive(CR[0], cx_s.at[0], cx_r.at[0], partner)
-    next(rf[0])
-    next(gf[1])
-    next(rf[0])
-    spread(1, F[1], PREV_F, SRC_F, 1)
+    run(rf[0], 1)
+    run(gf[1], 1)
+    spread(1, F[1], PREV_F, SRC_F, 1, 0, 96)
+    run(rf[0], 2)
+    spread(1, F[1], PREV_F, SRC_F, 1, 96)
     core_exchange(1)
-    next(rf[0])
-    next(rf[0])
+    run(rf[0], 1)
     arrive(CR[1], cx_s.at[1], cx_r.at[1], partner)
-    next(rf[1])
-    next(rf[1])
-    next(rf[0])
-    next(rf[1])
-    next(rf[1])
-    next(rf[1])
+    run(rf[1], 1)
+    run(rf[0], 1)
+    run(rf[1], 4)
 
     def own_tile(t, c):
         rows = pl.ds(pl.multiple_of(t * TILE, TILE), TILE)
@@ -275,12 +311,12 @@
 
     def from_partner(h):
         r = col_ring
-        places = [(r.i, r.p), (r.down, r.p), (r.up, r.p), (r.i, r.q), (r.far, r.p), (r.down, r.q), (r.up, r.q), (r.far, r.q)]
+        places = [(r.i, r.p), (r.i, r.q), (r.down, r.p), (r.up, r.p), (r.far, r.p), (r.down, r.q), (r.up, r.q), (r.far, r.q)]
         for n, (i, p) in enumerate(places):
             arrive(G[h].at[pl.ds((p * 8 + i * 2 + 1 - co) * OWN, OWN)], co_s.at[h, n], co_r.at[h, n], partner)
 
     def backward_term(h, i, p, t):
-        return S[h][table[LAST_B + (i * 2 + p) * OWN + t]]
+        return S[h][table[LAST_B, (i * 2 + p) * OWN + t]]
 
     def keep_feature_grad(h, t, value):
         feature_grad[t * TILE:(t + 1) * TILE, h * TILE:(h + 1) * TILE] = value.astype(BF16)
@@ -298,6 +334,7 @@
                 AGG[h][...], PG[...], (((0,), (0,)), ((), ())), preferred_element_type=F32
             )
 
+    def weight_send():
         def go(k, c):
             to = lax.rem(col + k, 16)
             send(WT.at[pl.ds(to * 16, 16)], WA.at[col], wa_s.at[k], wa_r.at[k], (row, to))
@@ -356,32 +393,33 @@
         lax.fori_loop(1, 16, got, 0)
         weight_grad[...] = WC[...]
 
-    next(gb[0])
+    run(gb[0], 1)
     weight_term()
-    next(gb[0])
-    next(gb[1])
-    next(gb[0])
-    next(gb[1])
-    next(gb[0])
+    run(gb[0], 2)
+    run(gb[1], 1)
+    weight_send()
+    run(gb[0], 2)
+    run(gb[1], 2)
+    run(gb[0], 1)
+    from_partner(0)
+    spread(0, G[0], PREV_B, SRC_B, 0, 0, 128)
+    run(gb[1], 1)
+    spread(0, G[0], PREV_B, SRC_B, 0, 128)
+    run(rb[0], 1)
     weight_row()
-    from_partner(0)
-    spread(0, G[0], PREV_B, SRC_B, 0)
-    next(gb[1])
-    next(rb[0])
+    run(gb[1], 2)
+    run(rb[0], 1)
+    from_partner(1)
+    run(rb[0], 1)
+    spread(1, G[1], PREV_B, SRC_B, 0, 0, 96)
+    run(rb[0], 1)
+    spread(1, G[1], PREV_B, SRC_B, 0, 96)
+    run(rb[1], 1)
     weight_back()
-    next(gb[1])
-    next(rb[0])
-    from_partner(1)
-    spread(1, G[1], PREV_B, SRC_B, 0)
-    next(rb[0])
-    next(rb[1])
-    next(rb[0])
-    next(rb[1])
-    next(rb[0])
-    next(rb[1])
-    next(rb[1])
+    run(rb[0], 1)
+    run(rb[1], 3)
     weight_end()
-    next(rb[1])
+    run(rb[1], 1)
 
     for copy in sent:
         copy.wait_send()
@@ -405,25 +443,23 @@
     lax.fori_loop(1, 8, gone_row, 0)
 
 
-def links(place, live, groups):
-    slot = jnp.arange(SLOTS, dtype=jnp.int32)
-    before = (place[None, :] == place[:, None]) & (slot[None, :] < slot[:, None]) & live[None, :]
-    previous = jnp.max(jnp.where(before, slot[None, :], -1), axis=1)
-    group = jnp.arange(groups, dtype=jnp.int32)
-    inside = (place[None, :] == group[:, None]) & live[None, :]
-    last = jnp.max(jnp.where(inside, slot[None, :], -1), axis=1)
-    return jnp.where(previous < 0, SLOTS, previous), jnp.where(last < 0, SLOTS, last)
+def copy_kernel(*refs):
+    count = len(refs) // 2
+    for n in range(count):
+        refs[count + n][...] = refs[n][...]
+
+
+def keep(*arrays):
+    where = pl.BlockSpec(memory_space=pltpu.VMEM)
+    return pl.pallas_call(
+        copy_kernel,
+        out_shape=tuple(jax.ShapeDtypeStruct(a.shape, a.dtype) for a in arrays),
+        in_specs=[where] * len(arrays),
+        out_specs=(where,) * len(arrays),
+    )(*arrays)
 
 
 def body(scaling, features, weight, tile_values, tile_coords, tile_counts, out_grad):
-    coords = tile_coords[0, 0]
-    live = jnp.arange(SLOTS, dtype=jnp.int32) < tile_counts[0, 0]
-    tile_row, tile_col = coords[:, 0], coords[:, 1]
-    prev_f, last_f = links(tile_row, live, ROW_TILES)
-    prev_b, last_b = links(tile_col, live, COL_TILES)
-    table = jnp.concatenate(
-        [prev_f, jnp.where(live, tile_col, 0), last_f, prev_b, jnp.where(live, tile_row, 0), last_b]
-    )
     rows, width = features.shape
     vmem = pl.BlockSpec(memory_space=pltpu.VMEM)
     tile = (TILE, TILE)
@@ -432,7 +468,7 @@
         return [pltpu.VMEM((count,) + tile, kind)] * 2
 
     dma = pltpu.SemaphoreType.DMA
-    return pl.pallas_call(
+    outs = pl.pallas_call(
         functools.partial(kernel, scaling),
         out_shape=(
             jax.ShapeDtypeStruct((rows, width), BF16),
@@ -440,7 +476,7 @@
             jax.ShapeDtypeStruct((rows, width), BF16),
         ),
         in_specs=[
-            pl.BlockSpec(memory_space=pltpu.SMEM), vmem, vmem, pl.BlockSpec(memory_space=pl.ANY), vmem,
+            pl.BlockSpec(memory_space=pltpu.SMEM), vmem, vmem, vmem, pl.BlockSpec(memory_space=pl.ANY), vmem,
         ],
         out_specs=(vmem, vmem, vmem),
         scratch_shapes=[
@@ -450,14 +486,16 @@
             pltpu.VMEM((rows, TILE), BF16), pltpu.VMEM((rows, TILE), BF16), pltpu.VMEM((rows, width), BF16),
             pltpu.VMEM((width, width), F32), pltpu.VMEM((16, 16, width), F32), pltpu.VMEM((16, width), F32),
             pltpu.VMEM((8, 16, width), F32), pltpu.VMEM((width, width), F32),
-            dma((4,)), dma((2, 9)), dma((2, 9)), dma((2,)), dma((2,)), dma((2, 9)), dma((2, 9)),
-            dma((2, 9)), dma((2, 9)), dma((2, 8)), dma((2, 8)), dma((2, 9)), dma((2, 9)),
+            pltpu.VMEM((8, WIDE), jnp.int32), pltpu.SMEM((8, WIDE), jnp.int32), dma(()),
+            dma((4,)), dma((2, 11)), dma((2, 11)), dma((2,)), dma((2,)), dma((2, 11)), dma((2, 11)),
+            dma((2, 11)), dma((2, 11)), dma((2, 8)), dma((2, 8)), dma((2, 11)), dma((2, 11)),
             dma((16,)), dma((16,)), dma((8,)), dma((8,)), dma((16,)), dma((16,)),
         ],
         compiler_params=pltpu.CompilerParams(
             collective_id=0, has_side_effects=True, vmem_limit_bytes=62 << 20
         ),
-    )(table, features, weight, tile_values[0, 0], out_grad)
+    )(tile_counts, tile_coords[0, 0].T, features, weight, tile_values[0, 0], out_grad)
+    return keep(*outs)
 
 
 def solution(mesh):

time: 115 us -> 102 us (0.89)
  local copies, waits for them, and re-layouts: 6.44 us -> 0 us
  Pallas kernels: 106 us -> 101 us
    pallas_call x1, Pallas kernels: 106 us -> 98.8 us  [body(): pl.pallas_call(functools.partial(kernel, scaling), out_shape=(jax.ShapeDt...]
    unnamed x3 -> x0, local copies, waits for them, and re-layouts: 5.01 us -> none
    pallas_call x0 -> x1, Pallas kernels: none -> 2 us  [keep(): pl.pallas_call(copy_kernel, out_shape=tuple((jax.ShapeDtypeStruct(a.shape...]
where the time goes in v2:
time: 102 us
  Pallas kernels  101 us (99%)
  between operations  1.29 us (1%)
    pallas_call x1, Pallas kernels, body(): pl.pallas_call(functools.partial(kernel, scaling), out_shape=(jax.ShapeDt...  98.8 us

profile of v2, /device:TPU:1, one launch (start us, length us, event | category | flops | bytes accessed | tf_op | source)
XLA Modules:
  0.0 102.1 jit_solution(7976544328545344561)
XLA Ops:
  1.3 98.8 %shard_map.85 = (bf16[512,256]{1,0:T(8,128)(2,1)}, f32[256,256]{1,0:T(8,128)}, bf16[512,256]{1,0:T(8,128)(2,1)}) custom-call(s32[1,1]{1,0:T(1,128)S(6)} %copy.9.count, s32[2,192]{1,0:T(2,128)} %bitcast.5, bf16[512,256]{1,0:T(8,128)(2,1)} %features.1, bf16[256,256]{1,0:T(8,128)(2,1)} %weight.1, bf16[192,128,128]{2,1,0:T(8,128)(2,1)} %bitcast.4, ...), custom_call_target="tpu_custom_call" | custom-call | tf_op jit(solution)/shard_map/pallas_call | solution.py:471
  100.1 2.0 %shard_map.86 = (bf16[512,256]{1,0:T(8,128)(2,1)}, f32[256,256]{1,0:T(8,128)}, bf16[512,256]{1,0:T(8,128)(2,1)}) custom-call(bf16[512,256]{1,0:T(8,128)(2,1)} %get-tuple-element.6.refs_0_, f32[256,256]{1,0:T(8,128)} %get-tuple-element.7.refs_1_, bf16[512,256]{1,0:T(8,128)(2,1)} %get-tuple-element.8.refs_2_), custom_call_target="tpu_custom_call" | custom-call | tf_op jit(solution)/shard_map/pallas_call | solution.py:454

commit v3 on v2

--- a/solution.py
+++ b/solution.py
@@ -182,11 +182,11 @@
 
 
 def kernel(
-    scaling, count, coords, features, weight, tiles, out_grad, activated, weight_grad, feature_grad,
+    scaling, count, coords, features, weight_hbm, tiles, out_grad_hbm, activated, weight_grad, feature_grad,
     T, S0, S1, F0, F1, CS0, CS1, CR0, CR1, AS0, AS1, AR0, AR1, G0, G1, BS0, BS1, BR0, BR1,
-    AGG0, AGG1, PG, WT, WA, WP, WB, WC,
-    TABLE, table, table_sem, tile_sem, gf_s, gf_r, cx_s, cx_r, rf_s, rf_r, gb_s, gb_r, co_s, co_r, rb_s, rb_r,
-    wa_s, wa_r, wb_s, wb_r, wc_s, wc_r,
+    AGG0, AGG1, PG, WT, WX, WS, WA, WP, WB, WC, weight, out_grad, ACT, FG,
+    TABLE, table, table_sem, own_sem, out_sem, tile_sem, gf_s, gf_r, cx_s, cx_r, rf_s, rf_r, gb_s, gb_r, co_s, co_r, rb_s, rb_r,
+    wx_s, wx_r, wa_s, wa_r, wb_s, wb_r, wc_s, wc_r,
 ):
     S, F, CS, CR, AS, AR = (S0, S1), (F0, F1), (CS0, CS1), (CR0, CR1), (AS0, AS1), (AR0, AR1)
     G, BS, BR, AGG = (G0, G1), (BS0, BS1), (BR0, BR1), (AGG0, AGG1)
@@ -198,32 +198,49 @@
     partner = (row, zh * 8 + y * 2 + 1 - co)
     sent = []
 
+    own_loads = []
+    for h in range(2):
+        for t in range(OWN):
+            own_loads.append(
+                pltpu.make_async_copy(
+                    features.at[pl.ds(t * TILE, TILE), pl.ds(h * TILE, TILE)], F[h].at[row * OWN + t],
+                    own_sem.at[h * OWN + t],
+                )
+            )
+            own_loads[-1].start()
     loads = []
     for n in range(4):
         span = pl.ds(n * (SLOTS // 4), SLOTS // 4)
         loads.append(pltpu.make_async_copy(tiles.at[span], T.at[span], tile_sem.at[n]))
         loads[-1].start()
 
+    for source, place in ((weight_hbm, weight), (out_grad_hbm, out_grad)):
+        loads.append(pltpu.make_async_copy(source, place, tile_sem.at[len(loads)]))
+        loads[-1].start()
+    stores = []
+
+    def store(source, place, n):
+        stores.append(pltpu.make_async_copy(source, place, out_sem.at[n]))
+        stores[-1].start()
+
     barrier = pltpu.get_barrier_semaphore()
 
-    def greet_col(k, c):
-        pl.semaphore_signal(barrier, inc=1, device_id=(row, lax.rem(col + k, 16)), device_id_type=MESH)
-        return c
-
-    def greet_row(k, c):
+    def greet(k, c):
+        near = (row, lax.rem(col + 2 * k, 16))
+        pl.semaphore_signal(barrier, inc=1, device_id=near, device_id_type=MESH)
         pl.semaphore_signal(barrier, inc=1, device_id=(lax.rem(row + k, 8), col), device_id_type=MESH)
         return c
 
-    lax.fori_loop(1, 16, greet_col, 0)
-    lax.fori_loop(1, 8, greet_row, 0)
+    pl.semaphore_signal(barrier, inc=1, device_id=partner, device_id_type=MESH)
+    lax.fori_loop(1, 8, greet, 0)
     for h in range(2):
-        for t in range(OWN):
-            F[h][row * OWN + t] = features[t * TILE:(t + 1) * TILE, h * TILE:(h + 1) * TILE]
         S[h][SLOTS] = jnp.zeros((TILE, TILE), F32)
     make_table(coords, count[0, 0], TABLE)
     table_copy = pltpu.make_async_copy(TABLE, table, table_sem)
     table_copy.start()
-    pl.semaphore_wait(barrier, 22)
+    for load in own_loads:
+        load.wait()
+    pl.semaphore_wait(barrier, 15)
 
     def spread(h, source, prev, src, contract, first=0, last=SLOTS):
         def step(k, c):
@@ -285,7 +302,7 @@
         pre = jnp.dot(AGG0[rows, :], weight[:TILE, :], preferred_element_type=F32)
         pre = pre + jnp.dot(AGG1[rows, :], weight[TILE:, :], preferred_element_type=F32)
         sigma = jax.nn.sigmoid(pre)
-        activated[rows, :] = (pre * sigma).astype(BF16)
+        ACT[rows, :] = (pre * sigma).astype(BF16)
         grad = out_grad[rows, :].astype(F32) * (sigma * (1.0 + pre * (1.0 - sigma)))
         grad = grad.astype(BF16)
         PG[rows, :] = grad
@@ -319,7 +336,7 @@
         return S[h][table[LAST_B, (i * 2 + p) * OWN + t]]
 
     def keep_feature_grad(h, t, value):
-        feature_grad[t * TILE:(t + 1) * TILE, h * TILE:(h + 1) * TILE] = value.astype(BF16)
+        FG[t * TILE:(t + 1) * TILE, h * TILE:(h + 1) * TILE] = value.astype(BF16)
 
     gb = [gather(col_ring, G[h], gb_s.at[h], gb_r.at[h], sent, to_partner(h)) for h in range(2)]
     rb = [
@@ -328,31 +345,40 @@
         for h in range(2)
     ]
 
+    chip = col // 2
+    half = pl.ds(pl.multiple_of(co * 128, 128), 128)
+    other = pl.ds(pl.multiple_of((1 - co) * 128, 128), 128)
+    here = pl.ds(pl.multiple_of(co * 128 + chip * 16, 16), 16)
+
     def weight_term():
         for h in range(2):
             WT[h * TILE:(h + 1) * TILE, :] = lax.dot_general(
                 AGG[h][...], PG[...], (((0,), (0,)), ((), ())), preferred_element_type=F32
             )
+        sent.append(send(WT.at[other], WX, wx_s.at[0], wx_r.at[0], partner))
 
     def weight_send():
+        arrive(WX, wx_s.at[0], wx_r.at[0], partner)
+        for n in range(8):
+            WS[n] = WT[pl.ds(pl.multiple_of(co * 128 + n * 16, 16), 16), :] + WX[n * 16:(n + 1) * 16, :]
+        WA[chip] = WS[chip]
+
         def go(k, c):
-            to = lax.rem(col + k, 16)
-            send(WT.at[pl.ds(to * 16, 16)], WA.at[col], wa_s.at[k], wa_r.at[k], (row, to))
-            return c
-
-        lax.fori_loop(1, 16, go, 0)
+            to = lax.rem(chip + k, 8)
+            send(WS.at[to], WA.at[chip], wa_s.at[k], wa_r.at[k], (row, to * 2 + co))
+            return c
+
+        lax.fori_loop(1, 8, go, 0)
 
     def weight_row():
-        WA[col] = WT[pl.ds(pl.multiple_of(col * 16, 16), 16), :]
-
         def got(k, c):
-            fro = lax.rem(col + 16 - k, 16)
-            arrive(WA.at[fro], wa_s.at[k], wa_r.at[k], (row, fro))
-            return c
-
-        lax.fori_loop(1, 16, got, 0)
+            fro = lax.rem(chip + 8 - k, 8)
+            arrive(WA.at[fro], wa_s.at[k], wa_r.at[k], (row, fro * 2 + co))
+            return c
+
+        lax.fori_loop(1, 8, got, 0)
         total = WA[0]
-        for n in range(1, 16):
+        for n in range(1, 8):
             total = total + WA[n]
         WP[...] = total
         WB[row] = total
@@ -374,26 +400,30 @@
         total = WB[0]
         for n in range(1, 8):
             total = total + WB[n]
-        here = pl.ds(pl.multiple_of(col * 16, 16), 16)
         WC[here, :] = total * scaling
 
         def go(k, c):
-            to = lax.rem(col + k, 16)
-            send(WC.at[here], WC.at[here], wc_s.at[k], wc_r.at[k], (row, to))
-            return c
-
-        lax.fori_loop(1, 16, go, 0)
+            to = lax.rem(chip + k, 8)
+            send(WC.at[here], WC.at[here], wc_s.at[k], wc_r.at[k], (row, to * 2 + co))
+            return c
+
+        lax.fori_loop(1, 8, go, 0)
+
+    def weight_share():
+        def got(k, c):
+            fro = lax.rem(chip + 8 - k, 8)
+            arrive(WC.at[pl.ds(co * 128 + fro * 16, 16)], wc_s.at[k], wc_r.at[k], (row, fro * 2 + co))
+            return c
+
+        lax.fori_loop(1, 8, got, 0)
+        sent.append(send(WC.at[half], WC.at[half], wx_s.at[1], wx_r.at[1], partner))
 
     def weight_end():
-        def got(k, c):
-            fro = lax.rem(col + 16 - k, 16)
-            arrive(WC.at[pl.ds(fro * 16, 16)], wc_s.at[k], wc_r.at[k], (row, fro))
-            return c
-
-        lax.fori_loop(1, 16, got, 0)
-        weight_grad[...] = WC[...]
+        arrive(WC.at[other], wx_s.at[1], wx_r.at[1], partner)
+        store(WC, weight_grad, 1)
 
     run(gb[0], 1)
+    store(ACT, activated, 0)
     weight_term()
     run(gb[0], 2)
     run(gb[1], 1)
@@ -417,30 +447,26 @@
     run(rb[1], 1)
     weight_back()
     run(rb[0], 1)
-    run(rb[1], 3)
+    run(rb[1], 1)
+    weight_share()
+    run(rb[1], 2)
     weight_end()
     run(rb[1], 1)
+    store(FG, feature_grad, 2)
+    for copy in stores:
+        copy.wait()
 
     for copy in sent:
         copy.wait_send()
 
-    def gone_col(k, c):
-        pltpu.make_async_remote_copy(
-            src_ref=WP, dst_ref=WP, send_sem=wa_s.at[k], recv_sem=wa_r.at[k], device_id=partner, device_id_type=MESH
-        ).wait_send()
-        pltpu.make_async_remote_copy(
-            src_ref=WP, dst_ref=WP, send_sem=wc_s.at[k], recv_sem=wc_r.at[k], device_id=partner, device_id_type=MESH
-        ).wait_send()
+    def gone(k, c):
+        for ss, rs in ((wa_s, wa_r), (wb_s, wb_r), (wc_s, wc_r)):
+            pltpu.make_async_remote_copy(
+                src_ref=WP, dst_ref=WP, send_sem=ss.at[k], recv_sem=rs.at[k], device_id=partner, device_id_type=MESH
+            ).wait_send()
         return c
 
-    def gone_row(k, c):
-        pltpu.make_async_remote_copy(
-            src_ref=WP, dst_ref=WP, send_sem=wb_s.at[k], recv_sem=wb_r.at[k], device_id=partner, device_id_type=MESH
-        ).wait_send()
-        return c
-
-    lax.fori_loop(1, 16, gone_col, 0)
-    lax.fori_loop(1, 8, gone_row, 0)
+    lax.fori_loop(1, 8, gone, 0)
 
 
 def copy_kernel(*refs):
@@ -461,7 +487,7 @@
 
 def body(scaling, features, weight, tile_values, tile_coords, tile_counts, out_grad):
     rows, width = features.shape
-    vmem = pl.BlockSpec(memory_space=pltpu.VMEM)
+    hbm = pl.BlockSpec(memory_space=pl.ANY)
     tile = (TILE, TILE)
 
     def twice(count, kind=BF16):
@@ -476,20 +502,22 @@
             jax.ShapeDtypeStruct((rows, width), BF16),
         ),
         in_specs=[
-            pl.BlockSpec(memory_space=pltpu.SMEM), vmem, vmem, vmem, pl.BlockSpec(memory_space=pl.ANY), vmem,
+            pl.BlockSpec(memory_space=pltpu.SMEM), pl.BlockSpec(memory_space=pltpu.VMEM), hbm, hbm, hbm, hbm,
         ],
-        out_specs=(vmem, vmem, vmem),
+        out_specs=(hbm, hbm, hbm),
         scratch_shapes=[
             pltpu.VMEM((SLOTS,) + tile, BF16),
             *twice(SLOTS + 1, F32), *twice(COL_TILES), *twice(32), *twice(32), *twice(R_TILES), *twice(R_TILES),
             *twice(ROW_TILES), *twice(R_TILES), *twice(R_TILES),
             pltpu.VMEM((rows, TILE), BF16), pltpu.VMEM((rows, TILE), BF16), pltpu.VMEM((rows, width), BF16),
-            pltpu.VMEM((width, width), F32), pltpu.VMEM((16, 16, width), F32), pltpu.VMEM((16, width), F32),
-            pltpu.VMEM((8, 16, width), F32), pltpu.VMEM((width, width), F32),
+            pltpu.VMEM((width, width), F32), pltpu.VMEM((width // 2, width), F32), pltpu.VMEM((8, 16, width), F32),
+            pltpu.VMEM((8, 16, width), F32), pltpu.VMEM((16, width), F32), pltpu.VMEM((8, 16, width), F32),
+            pltpu.VMEM((width, width), F32), pltpu.VMEM((width, width), BF16), pltpu.VMEM((rows, width), BF16),
+            pltpu.VMEM((rows, width), BF16), pltpu.VMEM((rows, width), BF16),
             pltpu.VMEM((8, WIDE), jnp.int32), pltpu.SMEM((8, WIDE), jnp.int32), dma(()),
-            dma((4,)), dma((2, 11)), dma((2, 11)), dma((2,)), dma((2,)), dma((2, 11)), dma((2, 11)),
+            dma((8,)), dma((3,)), dma((6,)), dma((2, 11)), dma((2, 11)), dma((2,)), dma((2,)), dma((2, 11)), dma((2, 11)),
             dma((2, 11)), dma((2, 11)), dma((2, 8)), dma((2, 8)), dma((2, 11)), dma((2, 11)),
-            dma((16,)), dma((16,)), dma((8,)), dma((8,)), dma((16,)), dma((16,)),
+            dma((2,)), dma((2,)), dma((8,)), dma((8,)), dma((8,)), dma((8,)), dma((8,)), dma((8,)),
         ],
         compiler_params=pltpu.CompilerParams(
             collective_id=0, has_side_effects=True, vmem_limit_bytes=62 << 20

time: 102 us -> 97.5 us (0.956)
  Pallas kernels: 101 us -> 96.1 us
    pallas_call x1, Pallas kernels: 98.8 us -> 94.1 us  [body(): pl.pallas_call(functools.partial(kernel, scaling), out_shape=(jax.ShapeDt...]
where the time goes in v3:
time: 97.5 us; the launch traced here: 97.4 us
  Pallas kernels  96.1 us (99%)
  between operations  1.29 us (1%)
    pallas_call x1, Pallas kernels, body(): pl.pallas_call(functools.partial(kernel, scaling), out_shape=(jax.ShapeDt...  94.1 us
    pallas_call x1, Pallas kernels, keep(): pl.pallas_call(copy_kernel, out_shape=tuple((jax.ShapeDtypeStruct(a.shape...  2 us

profile of v3, /device:TPU:1, one launch (start us, length us, event | category | flops | bytes accessed | tf_op | source)
XLA Modules:
  0.0 97.4 jit_solution(12092382593473751861)
XLA Ops:
  1.3 94.1 %shard_map.85 = (bf16[512,256]{1,0:T(8,128)(2,1)}, f32[256,256]{1,0:T(8,128)}, bf16[512,256]{1,0:T(8,128)(2,1)}) custom-call(s32[1,1]{1,0:T(1,128)S(6)} %copy.9.count, s32[2,192]{1,0:T(2,128)} %bitcast.5, bf16[512,256]{1,0:T(8,128)(2,1)} %features.1, bf16[256,256]{1,0:T(8,128)(2,1)} %weight_hbm.1, bf16[192,128,128]{2,1,0:T(8,128)(2,1)} %bitcast.4, ...), custom_call_target="tpu_custom_call" | custom-call | tf_op jit(solution)/shard_map/pallas_call | solution.py:497
  95.4 2.0 %shard_map.86 = (bf16[512,256]{1,0:T(8,128)(2,1)}, f32[256,256]{1,0:T(8,128)}, bf16[512,256]{1,0:T(8,128)(2,1)}) custom-call(bf16[512,256]{1,0:T(8,128)(2,1)} %get-tuple-element.6.refs_0_, f32[256,256]{1,0:T(8,128)} %get-tuple-element.7.refs_1_, bf16[512,256]{1,0:T(8,128)(2,1)} %get-tuple-element.8.refs_2_), custom_call_target="tpu_custom_call" | custom-call | tf_op jit(solution)/shard_map/pallas_call | solution.py:480

commit v4 on v3

--- a/solution.py
+++ b/solution.py
@@ -271,31 +271,26 @@
                AS[h], AR[h], rf_s.at[h], rf_r.at[h], sent)
         for h in range(2)
     ]
-    run(gf[0], 3)
-    run(gf[1], 1)
-    run(gf[0], 2)
-    run(gf[1], 2)
-    run(gf[0], 1)
-    table_copy.wait()
-    for load in loads:
-        load.wait()
-    spread(0, F[0], PREV_F, SRC_F, 1, 0, 128)
-    run(gf[1], 1)
-    spread(0, F[0], PREV_F, SRC_F, 1, 128)
-    core_exchange(0)
-    run(gf[1], 1)
-    arrive(CR[0], cx_s.at[0], cx_r.at[0], partner)
-    run(rf[0], 1)
-    run(gf[1], 1)
-    spread(1, F[1], PREV_F, SRC_F, 1, 0, 96)
-    run(rf[0], 2)
-    spread(1, F[1], PREV_F, SRC_F, 1, 96)
-    core_exchange(1)
-    run(rf[0], 1)
-    arrive(CR[1], cx_s.at[1], cx_r.at[1], partner)
-    run(rf[1], 1)
-    run(rf[0], 1)
-    run(rf[1], 4)
+    def products(h, first, last):
+        if first == 0 and h == 0:
+            table_copy.wait()
+            for load in loads:
+                load.wait()
+        spread(h, F[h], PREV_F, SRC_F, 1, first, last)
+
+    def from_core(h):
+        arrive(CR[h], cx_s.at[h], cx_r.at[h], partner)
+
+    f0, f1 = functools.partial(run, gf[0], 1), functools.partial(run, gf[1], 1)
+    r0, r1 = functools.partial(run, rf[0], 1), functools.partial(run, rf[1], 1)
+    p0 = functools.partial(products, 0, 0, SLOTS)
+    p1a, p1b = functools.partial(products, 1, 0, SLOTS // 2), functools.partial(products, 1, SLOTS // 2, SLOTS)
+    c0, c1 = functools.partial(core_exchange, 0), functools.partial(core_exchange, 1)
+    w0, w1 = functools.partial(from_core, 0), functools.partial(from_core, 1)
+    for step in (
+        f0, f1, f0, f1, f0, f0, f0, f1, f1, f0, p0, c0, f1, f1, p1a, w0, r0, p1b, c1, w1, r1, r0, r0, r1, r1, r0, r1, r0, r1,
+    ):
+        step()
 
     def own_tile(t, c):
         rows = pl.ds(pl.multiple_of(t * TILE, TILE), TILE)
@@ -422,36 +417,22 @@
         arrive(WC.at[other], wx_s.at[1], wx_r.at[1], partner)
         store(WC, weight_grad, 1)
 
-    run(gb[0], 1)
     store(ACT, activated, 0)
-    weight_term()
-    run(gb[0], 2)
-    run(gb[1], 1)
-    weight_send()
-    run(gb[0], 2)
-    run(gb[1], 2)
-    run(gb[0], 1)
-    from_partner(0)
-    spread(0, G[0], PREV_B, SRC_B, 0, 0, 128)
-    run(gb[1], 1)
-    spread(0, G[0], PREV_B, SRC_B, 0, 128)
-    run(rb[0], 1)
-    weight_row()
-    run(gb[1], 2)
-    run(rb[0], 1)
-    from_partner(1)
-    run(rb[0], 1)
-    spread(1, G[1], PREV_B, SRC_B, 0, 0, 96)
-    run(rb[0], 1)
-    spread(1, G[1], PREV_B, SRC_B, 0, 96)
-    run(rb[1], 1)
-    weight_back()
-    run(rb[0], 1)
-    run(rb[1], 1)
-    weight_share()
-    run(rb[1], 2)
-    weight_end()
-    run(rb[1], 1)
+
+    def back_products(h, first, last):
+        spread(h, G[h], PREV_B, SRC_B, 0, first, last)
+
+    g0, g1 = functools.partial(run, gb[0], 1), functools.partial(run, gb[1], 1)
+    r0, r1 = functools.partial(run, rb[0], 1), functools.partial(run, rb[1], 1)
+    q0, q1 = functools.partial(from_partner, 0), functools.partial(from_partner, 1)
+    a0, b0 = functools.partial(back_products, 0, 0, SLOTS // 2), functools.partial(back_products, 0, SLOTS // 2, SLOTS)
+    a1, b1 = functools.partial(back_products, 1, 0, SLOTS // 2), functools.partial(back_products, 1, SLOTS // 2, SLOTS)
+    wt, ws, wr, wb, wh, we = weight_term, weight_send, weight_row, weight_back, weight_share, weight_end
+    for step in (
+        g0, g0, g1, g0, wt, g0, g1, ws, g0, g1, g0, g1, q0, a0, b0, r0, g1, g1, wr, q1, a1, b1,
+        r0, r1, r0, r1, wb, r0, r1, r1, wh, we, r0, r1,
+    ):
+        step()
     store(FG, feature_grad, 2)
     for copy in stores:
         copy.wait()

time: 97.5 us -> 91.4 us (0.937)
  Pallas kernels: 96.1 us -> 89.9 us
    pallas_call x1, Pallas kernels: 94.1 us -> 87.9 us  [body(): pl.pallas_call(functools.partial(kernel, scaling), out_shape=(jax.ShapeDt...]
where the time goes in v4:
time: 91.4 us; the launch traced here: 91.2 us
  Pallas kernels  89.9 us (98%)
  between operations  1.29 us (1%)
    pallas_call x1, Pallas kernels, body(): pl.pallas_call(functools.partial(kernel, scaling), out_shape=(jax.ShapeDt...  87.9 us
    pallas_call x1, Pallas kernels, keep(): pl.pallas_call(copy_kernel, out_shape=tuple((jax.ShapeDtypeStruct(a.shape...  2 us

profile of v4, /device:TPU:1, one launch (start us, length us, event | category | flops | bytes accessed | tf_op | source)
XLA Modules:
  0.0 91.2 jit_solution(18385506433658000556)
XLA Ops:
  1.3 87.9 %shard_map.85 = (bf16[512,256]{1,0:T(8,128)(2,1)}, f32[256,256]{1,0:T(8,128)}, bf16[512,256]{1,0:T(8,128)(2,1)}) custom-call(s32[1,1]{1,0:T(1,128)S(6)} %copy.9.count, s32[2,192]{1,0:T(2,128)} %bitcast.5, bf16[512,256]{1,0:T(8,128)(2,1)} %features.1, bf16[256,256]{1,0:T(8,128)(2,1)} %weight_hbm.1, bf16[192,128,128]{2,1,0:T(8,128)(2,1)} %bitcast.4, ...), custom_call_target="tpu_custom_call" | custom-call | tf_op jit(solution)/shard_map/pallas_call | solution.py:478
  89.2 2.0 %shard_map.86 = (bf16[512,256]{1,0:T(8,128)(2,1)}, f32[256,256]{1,0:T(8,128)}, bf16[512,256]{1,0:T(8,128)(2,1)}) custom-call(bf16[512,256]{1,0:T(8,128)(2,1)} %get-tuple-element.6.refs_0_, f32[256,256]{1,0:T(8,128)} %get-tuple-element.7.refs_1_, bf16[512,256]{1,0:T(8,128)(2,1)} %get-tuple-element.8.refs_2_), custom_call_target="tpu_custom_call" | custom-call | tf_op jit(solution)/shard_map/pallas_call | solution.py:461

commit v5 on v4

--- a/solution.py
+++ b/solution.py
@@ -99,7 +99,7 @@
     yield
 
 
-def reduce(ring, partial, out, sbuf, rbuf, ss, rs, sent):
+def reduce(ring, partial, out, sbuf, rbuf, ss, rs, sent, ready=lambda: None):
     i, p, q, up, down, far = ring.i, ring.p, ring.q, ring.up, ring.down, ring.far
 
     def go(n, first, count, device):
@@ -124,6 +124,7 @@
     go(2, R_NEARP_U, OWN, ring.d_up)
     put(R_NEARP_D, (down, q))
     go(3, R_NEARP_D, OWN, ring.d_down)
+    ready()
     put(R_NEAR_U + HALF, (up, p), (2, 3))
     go(4, R_NEAR_U + HALF, HALF, ring.d_up)
     put(R_NEAR_D, (down, p), (0, 1))
@@ -250,13 +251,16 @@
             S[h][k] = S[h][table[prev, k]] + term
             return c
 
-        lax.fori_loop(first, last, step, 0, unroll=32)
+        lax.fori_loop(first, last, step, 0, unroll=48)
 
     def core_exchange(h):
-        for b in range(8):
-            for t in range(OWN):
-                CS[h][b * OWN + t] = S[h][table[LAST_F, (b * 2 + 1 - co) * OWN + t]].astype(BF16)
-        sent.append(send(CS[h], CR[h], cx_s.at[h], cx_r.at[h], partner))
+        for n, p in enumerate((1 - zh, zh)):
+            for b in range(4):
+                for t in range(OWN):
+                    place = p * 4 + b
+                    CS[h][place * OWN + t] = S[h][table[LAST_F, (place * 2 + 1 - co) * OWN + t]].astype(BF16)
+            span = pl.ds(p * 16, 16)
+            sent.append(send(CS[h].at[span], CR[h].at[span], cx_s.at[h, n], cx_r.at[h, n], partner))
 
     def forward_term(h, i, p, t):
         b = p * 4 + i
@@ -265,10 +269,16 @@
     def keep_aggregated(h, t, value):
         AGG[h][t * TILE:(t + 1) * TILE, :] = value.astype(BF16)
 
+    def from_core(h):
+        arrive(CR[h].at[pl.ds((1 - zh) * 16, 16)], cx_s.at[h, 0], cx_r.at[h, 0], partner)
+
+    def from_core_rest(h):
+        arrive(CR[h].at[pl.ds(zh * 16, 16)], cx_s.at[h, 1], cx_r.at[h, 1], partner)
+
     gf = [gather(row_ring, F[h], gf_s.at[h], gf_r.at[h], sent) for h in range(2)]
     rf = [
         reduce(col_ring, functools.partial(forward_term, h), functools.partial(keep_aggregated, h),
-               AS[h], AR[h], rf_s.at[h], rf_r.at[h], sent)
+               AS[h], AR[h], rf_s.at[h], rf_r.at[h], sent, functools.partial(from_core_rest, h))
         for h in range(2)
     ]
     def products(h, first, last):
@@ -277,9 +287,6 @@
             for load in loads:
                 load.wait()
         spread(h, F[h], PREV_F, SRC_F, 1, first, last)
-
-    def from_core(h):
-        arrive(CR[h], cx_s.at[h], cx_r.at[h], partner)
 
     f0, f1 = functools.partial(run, gf[0], 1), functools.partial(run, gf[1], 1)
     r0, r1 = functools.partial(run, rf[0], 1), functools.partial(run, rf[1], 1)
@@ -496,7 +503,7 @@
             pltpu.VMEM((width, width), F32), pltpu.VMEM((width, width), BF16), pltpu.VMEM((rows, width), BF16),
             pltpu.VMEM((rows, width), BF16), pltpu.VMEM((rows, width), BF16),
             pltpu.VMEM((8, WIDE), jnp.int32), pltpu.SMEM((8, WIDE), jnp.int32), dma(()),
-            dma((8,)), dma((3,)), dma((6,)), dma((2, 11)), dma((2, 11)), dma((2,)), dma((2,)), dma((2, 11)), dma((2, 11)),
+            dma((8,)), dma((3,)), dma((6,)), dma((2, 11)), dma((2, 11)), dma((2, 2)), dma((2, 2)), dma((2, 11)), dma((2, 11)),
             dma((2, 11)), dma((2, 11)), dma((2, 8)), dma((2, 8)), dma((2, 11)), dma((2, 11)),
             dma((2,)), dma((2,)), dma((8,)), dma((8,)), dma((8,)), dma((8,)), dma((8,)), dma((8,)),
         ],

time: 91.4 us -> 90.8 us (level)
  no operation moved by 1% of the time
where the time goes in v5:
time: 90.8 us; the launch traced here: 90.6 us
  Pallas kernels  89.3 us (98%)
  between operations  1.29 us (1%)
    pallas_call x1, Pallas kernels, body(): pl.pallas_call(functools.partial(kernel, scaling), out_shape=(jax.ShapeDt...  87.3 us
    pallas_call x1, Pallas kernels, keep(): pl.pallas_call(copy_kernel, out_shape=tuple((jax.ShapeDtypeStruct(a.shape...  2 us

profile of v5, /device:TPU:1, one launch (start us, length us, event | category | flops | bytes accessed | tf_op | source)
XLA Modules:
  0.0 90.6 jit_solution(18291158987845434100)
XLA Ops:
  1.3 87.3 %shard_map.85 = (bf16[512,256]{1,0:T(8,128)(2,1)}, f32[256,256]{1,0:T(8,128)}, bf16[512,256]{1,0:T(8,128)(2,1)}) custom-call(s32[1,1]{1,0:T(1,128)S(6)} %copy.9.count, s32[2,192]{1,0:T(2,128)} %bitcast.5, bf16[512,256]{1,0:T(8,128)(2,1)} %features.1, bf16[256,256]{1,0:T(8,128)(2,1)} %weight_hbm.1, bf16[192,128,128]{2,1,0:T(8,128)(2,1)} %bitcast.4, ...), custom_call_target="tpu_custom_call" | custom-call | tf_op jit(solution)/shard_map/pallas_call | solution.py:485
  88.6 2.0 %shard_map.86 = (bf16[512,256]{1,0:T(8,128)(2,1)}, f32[256,256]{1,0:T(8,128)}, bf16[512,256]{1,0:T(8,128)(2,1)}) custom-call(bf16[512,256]{1,0:T(8,128)(2,1)} %get-tuple-element.6.refs_0_, f32[256,256]{1,0:T(8,128)} %get-tuple-element.7.refs_1_, bf16[512,256]{1,0:T(8,128)(2,1)} %get-tuple-element.8.refs_2_), custom_call_target="tpu_custom_call" | custom-call | tf_op jit(solution)/shard_map/pallas_call | solution.py:468
